TPU v7x, 512 devices: a whole 4x8x8 slice. The times are simulated.
512 devices in a mesh: section: 4 (over x), seq: 128 (over z, y, core).
Axes of the slice: x: 4, y: 8, z: 8, core: 2. Of those that a mesh axis runs over, the one named last changes fastest.
Arguments:
- hidden: bfloat16 [65536, 4096], P('seq', 'section'), may hold values from -6 to 6
- norm_gain: bfloat16 [4096], P('section'), may hold values from 0.25 to 1.75
- query_weight: bfloat16 [4096, 512], P(None, 'section')
- key_weight: bfloat16 [4096, 128], P('section')
- value_weight: bfloat16 [4096, 128], P('section'), may hold values from -0.5 to 0.5
- output_weight: bfloat16 [512, 4096], P(None, 'section'), may hold values from -0.25 to 0.25
- block_reach: int32 [512], P('seq'), may hold values from 0 to 2
- header_ids: int32 [2], replicated, may hold values from 0 to 511, as said below
Outputs:
- attention_out: bfloat16 [65536, 4096], P('seq', 'section')
Inputs may be any that keep to these rules, and one draw needn't show every extreme that they name: `header_ids`: the 2 indices are distinct block indices, and the last block, 511, is always one of them, at any position.
All inputs are finite; a program needn't handle non-finite values.
Results may differ from a plain program's by a relative error of at most 0.014.
Values may be sent and summed in bfloat16 or wider, within the bound.
No kernel may reach another device: no remote copies, remote signals or barrier semaphores. Data moves between devices by JAX's collectives and lax.ppermute only.
A program may use at most 64 MiB of HBM per device.

v0:
```python
import math
import jax
import jax.numpy as jnp
from jax import lax
from jax.sharding import PartitionSpec as P

BLOCK = 128
REACH = 2
EPSILON = 1e-05
THETA = 500000.0


def merged(value, axis, combine):
    everything = jax.tree.map(lambda part: lax.all_gather(part, axis), value)
    leading = jax.tree.map(lambda part: part[0], everything)

    def lap(k, so_far):
        return combine(so_far, jax.tree.map(lambda part: part[k], everything))

    return lax.fori_loop(1, lax.axis_size(axis), lap, leading)


def padded(cells, sides, width):
    for axis, dim in sides:
        count = lax.axis_size(axis)
        ends = count - 1
        head = lax.slice_in_dim(cells, 0, width, axis=dim)
        tail = lax.slice_in_dim(cells, cells.shape[dim] - width, cells.shape[dim], axis=dim)
        cells = jnp.concatenate(
            [
                lax.ppermute(tail, axis, [(i, (i + 1) % count) for i in range(ends)]),
                cells,
                lax.ppermute(head, axis, [((i + 1) % count, i) for i in range(ends)]),
            ],
            axis=dim,
        )
    return cells


def tables(positions, head_width):
    middle = head_width // 2
    frequency = jnp.exp(
        -(2.0 / head_width) * math.log(THETA) * jnp.arange(middle, dtype=jnp.float32)
    )
    angles = positions.astype(jnp.float32)[:, None] * frequency[None, :]
    angles = jnp.concatenate([angles, angles], axis=1)
    return (jnp.cos(angles), jnp.sin(angles))


def rotate(values, cosine_table, sine_table):
    middle = values.shape[-1] // 2
    turned = jnp.concatenate([-values[..., middle:], values[..., :middle]], axis=-1)
    return values * cosine_table + turned * sine_table


def combine_parts(earlier, later):
    first_max, first_total, first_out = earlier
    second_max, second_total, second_out = later
    overall = jnp.maximum(first_max, second_max)
    first_factor = jnp.exp(first_max - overall)
    second_factor = jnp.exp(second_max - overall)
    return (
        overall,
        first_total * first_factor + second_total * second_factor,
        first_out * first_factor[:, None] + second_out * second_factor[:, None],
    )


def on_device(
    hidden,
    norm_gain,
    query_weight,
    key_weight,
    value_weight,
    output_weight,
    block_reach,
    header_ids,
):
    row_count = hidden.shape[0]
    part_width = hidden.shape[1]
    head_width = key_weight.shape[1]
    local_blocks = row_count // BLOCK
    total_blocks = local_blocks * lax.axis_size("seq")
    seq_place = lax.axis_index("seq")
    floats = hidden.astype(jnp.float32)
    squares = lax.psum(jnp.sum(floats * floats, axis=1), "section")
    scaling = lax.rsqrt(squares / (part_width * lax.axis_size("section")) + EPSILON)
    normed_part = (floats * scaling[:, None] * norm_gain.astype(jnp.float32)[None, :]).astype(
        jnp.bfloat16
    )
    weight_rows = query_weight
    query_sum = jnp.dot(
        lax.all_gather(normed_part, "section", axis=1, tiled=True),
        weight_rows,
        preferred_element_type=jnp.float32,
    )
    key_sum, value_sum = lax.psum(
        (
            jnp.dot(normed_part, key_weight, preferred_element_type=jnp.float32),
            jnp.dot(normed_part, value_weight, preferred_element_type=jnp.float32),
        ),
        "section",
    )
    positions = seq_place * row_count + jnp.arange(row_count, dtype=jnp.int32)
    cosine_table, sine_table = tables(positions, head_width)
    queries = rotate(query_sum, cosine_table, sine_table).astype(jnp.bfloat16)
    keys_here = rotate(key_sum, cosine_table, sine_table).astype(jnp.bfloat16)
    values_here = value_sum.astype(jnp.bfloat16)
    packed = jnp.concatenate([queries, keys_here, values_here], axis=1)
    block_numbers = seq_place * local_blocks + jnp.arange(local_blocks, dtype=jnp.int32)
    select = header_ids[:, None] == block_numbers[None, :]
    shaped = packed.reshape(local_blocks, BLOCK, 3 * head_width)
    picked = jnp.einsum(
        "hb,bre->hre", select.astype(jnp.bfloat16), shaped, preferred_element_type=jnp.float32
    )
    header_pack = lax.psum(picked, "seq").astype(jnp.bfloat16).reshape(-1, 3 * head_width)
    head_queries = header_pack[:, :head_width]
    head_keys = header_pack[:, head_width : 2 * head_width]
    head_values = header_pack[:, 2 * head_width :]
    inverse_root = 1.0 / math.sqrt(head_width)
    far_scores = (
        jnp.einsum("qd,kd->qk", head_queries, keys_here, preferred_element_type=jnp.float32)
        * inverse_root
    )
    far_max = jnp.max(far_scores, axis=1)
    far_weights = jnp.exp(far_scores - far_max[:, None])
    far_total = jnp.sum(far_weights, axis=1)
    far_out = jnp.dot(
        far_weights.astype(jnp.bfloat16), values_here, preferred_element_type=jnp.float32
    )
    merged_max, merged_total, merged_out = merged(
        (far_max, far_total, far_out), "seq", combine_parts
    )
    header_result = merged_out / merged_total[:, None]
    margin_rows = REACH * BLOCK
    stacked = jnp.concatenate([keys_here, values_here], axis=1)
    extended = padded(stacked, (("seq", 0),), margin_rows)
    near_keys = extended[:, :head_width]
    near_values = extended[:, head_width:]
    extent = row_count + 2 * margin_rows
    key_blocks = seq_place * local_blocks - REACH + jnp.arange(extent, dtype=jnp.int32) // BLOCK
    query_blocks = seq_place * local_blocks + jnp.arange(row_count, dtype=jnp.int32) // BLOCK
    limits = jnp.repeat(block_reach, BLOCK)
    key_header = jnp.any(header_ids[:, None] == key_blocks[None, :], axis=0)
    allowed = (key_blocks >= 0)[None, :] & (key_blocks < total_blocks)[None, :]
    allowed = allowed & (jnp.abs(key_blocks[None, :] - query_blocks[:, None]) <= limits[:, None])
    allowed = allowed & jnp.logical_not(key_header)[None, :]
    near_scores = (
        jnp.einsum("qd,kd->qk", queries, near_keys, preferred_element_type=jnp.float32)
        * inverse_root
    )
    near_scores = jnp.where(allowed, near_scores, -jnp.inf)
    head_scores = (
        jnp.einsum("qd,kd->qk", queries, head_keys, preferred_element_type=jnp.float32)
        * inverse_root
    )
    scores = jnp.concatenate([near_scores, head_scores], axis=1)
    row_top = jnp.max(scores, axis=1)
    weights = jnp.exp(scores - row_top[:, None])
    row_sums = jnp.sum(weights, axis=1)
    joined = jnp.concatenate([near_values, head_values], axis=0)
    mixed_out = (
        jnp.dot(weights.astype(jnp.bfloat16), joined, preferred_element_type=jnp.float32)
        / row_sums[:, None]
    )
    header_local = jnp.einsum(
        "hb,hre->bre", select.astype(jnp.float32), header_result.reshape(-1, BLOCK, head_width)
    )
    is_local_header = jnp.any(select, axis=0)
    attended = jnp.where(
        is_local_header[:, None, None],
        header_local,
        mixed_out.reshape(local_blocks, BLOCK, head_width),
    )
    attended = attended.reshape(row_count, head_width).astype(jnp.bfloat16)
    weight_rows = output_weight
    result = jnp.dot(
        lax.all_gather(attended, "section", axis=1, tiled=True),
        weight_rows,
        preferred_element_type=jnp.float32,
    )
    return result.astype(jnp.bfloat16)


def solution(mesh):
    return jax.shard_map(
        on_device,
        mesh=mesh,
        in_specs=(
            P("seq", "section"),
            P("section"),
            P(None, "section"),
            P("section", None),
            P("section", None),
            P(None, "section"),
            P("seq"),
            P(),
        ),
        out_specs=P("seq", "section"),
        check_vma=False,
    )
```

profile of v0, /device:TPU:64, one launch (start us, length us, event | category | flops | bytes accessed | tf_op | source)
XLA Modules:
  0.0 913.6 jit_solution(16988144689448362159)
XLA Ops:
  7.3 1.5 fusion.2
  8.8 10.5 %psum.28 = f32[512]{0:T(512)S(1)} all-reduce(f32[512]{0:T(512)S(1)} %fusion.2), channel_id=1, replica_groups=mesh['section'=4,'seq'=128] {'section'}, use_global_device_ids=true, to_apply=%region_2.0 | all-reduce | flops 512 | bytes 4096 | tf_op jit(solution)/shard_map/psum | solution.py:86
  19.3 1.6 fusion.4
  20.9 1.2 fusion.53
  23.0 1.7 fusion.54
  24.8 17.2 %all-reduce.5 = bf16[512,128]{0,1:T(8,128)(2,1)S(1)} all-reduce(f32[512,128]{0,1:T(8,128)S(1)} %fusion.54), channel_id=1, replica_groups=mesh['section'=4,'seq'=128] {'section'}, use_global_device_ids=true, to_apply=%region_4.0 | all-reduce | flops 65536 | bytes 393216 | tf_op jit(solution)/shard_map/psum | solution.py:97
  42.0 34.5 %all-reduce.4.cloned.1.call-done = f32[512,128]{0,1:T(8,128)} async-done(((f32[512,128]{0,1:T(8,128)}), f32[512,128]{0,1:T(8,128)}) %all-reduce.4.cloned.1.call-update) | async-done | bytes 262160 | tf_op jit(solution)/shard_map/psum | solution.py:97
  77.5 55.5 %all-gather.8.cloned.1.call-done = bf16[512,4096]{1,0:T(8,128)(2,1)} async-done(((bf16[512,1024]{1,0:T(8,128)(2,1)}), bf16[512,4096]{1,0:T(8,128)(2,1)}) %all-gather.8.cloned.1.call-update) | async-done | bytes 4194320 | tf_op jit(solution)/shard_map/all_gather | solution.py:93
  133.0 3.7 fusion.52
  138.7 461.0 %all-reduce.6 = bf16[2,128,384]{2,0,1:T(2,128)(2,1)S(1)} all-reduce(f32[2,128,384]{2,0,1:T(2,128)S(1)} %fusion.48), channel_id=1, replica_groups=mesh['section'=4,'seq'=128] {'seq'}, use_global_device_ids=true, to_apply=%region_5.0 | all-reduce | flops 98304 | bytes 589824 | tf_op jit(solution)/shard_map/psum | solution.py:116
  601.6 82.4 %all-gather.3 = f32[128,1,256]{2,1,0:T(1,128)S(1)} all-gather(f32[1,1,256]{2,1,0:T(1,128)S(1)} %bitcast.66), channel_id=2, replica_groups=mesh['section'=4,'seq'=128] {'seq'}, dimensions={0}, use_global_device_ids=true | all-gather | bytes 132096 | tf_op jit(solution)/shard_map/all_gather | solution.py:14
  684.3 47.1 %all-gather.4 = f32[128,1,256]{2,1,0:T(1,128)S(1)} all-gather(f32[1,1,256]{2,1,0:T(1,128)S(1)} %bitcast.67), channel_id=3, replica_groups=mesh['section'=4,'seq'=128] {'seq'}, dimensions={0}, use_global_device_ids=true | all-gather | bytes 132096 | tf_op jit(solution)/shard_map/all_gather | solution.py:14
  731.4 4.6 collective-permute-start.1
  736.0 1.9 collective-permute-start
  738.5 5.9 collective-permute-done
  748.1 144.2 %while.19 = (s32[]{:T(128)}, f32[256]{0:T(256)S(1)}, f32[256]{0:T(256)S(1)}, f32[256,128]{1,0:T(8,128)S(1)}, f32[128,256]{1,0:T(8,128)S(1)}, /*index=5*/f32[128,...) while((s32[]{:T(128)}, f32[256]{0:T(256)S(1)}, f32[256]{0:T(256)S(1)}, ...), condition=%wide.region_9.10_spmd, body=%wide.region_8.0_spmd.sunk | while | flops 99845 | bytes 407703 | solution.py:20
  749.3 1.1 fusion.69
  751.5 1.1 fusion.69
  753.8 1.1 fusion.69
  754.9 1.1 fusion.69
  756.1 1.1 fusion.69
  757.2 1.1 fusion.69
  758.3 1.1 fusion.69
  759.5 1.1 fusion.69
  761.7 1.1 fusion.69
  764.0 1.1 fusion.69
  766.3 1.1 fusion.69
  768.6 1.1 fusion.69
  770.8 1.1 fusion.69
  773.1 1.1 fusion.69
  775.4 1.1 fusion.69
  776.5 1.1 fusion.69
  777.6 1.1 fusion.69
  778.8 1.1 fusion.69
  779.9 1.1 fusion.69
  781.1 1.1 fusion.69
  783.3 1.1 fusion.69
  785.6 1.1 fusion.69
  787.9 1.1 fusion.69
  790.1 1.1 fusion.69
  792.4 1.1 fusion.69
  794.7 1.1 fusion.69
  797.0 1.1 fusion.69
  798.1 1.1 fusion.69
  799.2 1.1 fusion.69
  800.4 1.1 fusion.69
  892.8 12.6 %all_gather.31 = bf16[512,512]{1,0:T(8,128)(2,1)S(1)} all-gather(bf16[512,128]{1,0:T(8,128)(2,1)S(1)} %bitcast.59), channel_id=1, replica_groups=mesh['section'=4,'seq'=128] {'section'}, dimensions={1}, use_global_device_ids=true | all-gather | bytes 655360 | tf_op jit(solution)/shard_map/all_gather | solution.py:178
  905.4 1.7 convolution_convert_fusion
  (426 shorter events, 119.3 us)
Async XLA Ops:
  6.5 898.9 %copy-start = (bf16[512,1024]{1,0:T(8,128)(2,1)S(1)}, bf16[512,1024]{1,0:T(8,128)(2,1)}, u32[]{:S(2)}) copy-start(bf16[512,1024]{1,0:T(8,128)(2,1)} %param.15) | copy-start | bytes 3145732
  6.5 14.4 %copy-start.7 = (bf16[1024,128]{1,0:T(8,128)(2,1)S(1)}, bf16[1024,128]{1,0:T(8,128)(2,1)}, u32[]{:S(2)}) copy-start(bf16[1024,128]{1,0:T(8,128)(2,1)} %param.13) | copy-start | bytes 786436
  6.5 70.0 %all-reduce.4.cloned.1.call-start = ((), (), s32[]{:S(2)}) async-start(), calls=%async_computation.1 | async-start | bytes 524288 | tf_op jit(solution)/shard_map/psum | solution.py:97
  19.3 3.6 copy-start.8
  20.9 1.3 copy-start.1
  22.1 110.9 %copy-start.4 = (bf16[4096,128]{1,0:T(8,128)(2,1)S(1)}, bf16[4096,128]{1,0:T(8,128)(2,1)}, u32[]{:S(2)}) copy-start(bf16[4096,128]{1,0:T(8,128)(2,1)} %param.12) | copy-start | bytes 3145732
  22.2 110.8 %all-gather.8.cloned.1.call-start = ((), (), s32[]{:S(2)}) async-start(), calls=%async_computation | async-start | bytes 5242880 | tf_op jit(solution)/shard_map/all_gather | solution.py:93
  22.9 724.2 %all-gather.10.cloned.1.call-start = ((), (), s32[]{:S(2)}) async-start(), calls=%async_computation.2 | async-start | bytes 16908288 | tf_op jit(solution)/shard_map/all_gather | solution.py:14
  77.5 59.2 %copy-start.3 = (f32[512,128]{0,1:T(8,128)S(1)}, f32[512,128]{0,1:T(8,128)}, u32[]{:S(2)}) copy-start(f32[512,128]{0,1:T(8,128)} %all-reduce.4.cloned.1.call-done) | copy-start | bytes 786436
  136.7 1.6 copy-start.9
  138.3 463.3 %copy-start.10 = (s32[4]{0:T(128)S(1)}, s32[4]{0:T(128)}, u32[]{:S(2)}) copy-start(s32[4]{0:T(128)} %param.16) | copy-start | bytes 52
  684.1 61.5 %copy-start.6 = (f32[128,1,256]{2,1,0:T(1,128)}, f32[128,1,256]{2,1,0:T(1,128)S(1)}, u32[]{:S(2)}) copy-start(f32[128,1,256]{2,1,0:T(1,128)S(1)} %all-gather.3) | copy-start | bytes 393220
  731.4 14.1 %copy-start.5 = (f32[128,1,256]{2,1,0:T(1,128)}, f32[128,1,256]{2,1,0:T(1,128)S(1)}, u32[]{:S(2)}) copy-start(f32[128,1,256]{2,1,0:T(1,128)S(1)} %all-gather.4) | copy-start | bytes 393220
  731.4 7.1 collective-permute-start.1
  736.0 8.4 collective-permute-start
  744.5 1.1 copy-start.2
  745.6 1.0 slice-start
  746.5 1.5 slice-start.1
  746.5 1.5 slice-start.2
Sparse Core Ops, SparseCore 0:
  22.3 54.2 all-reduce.3
  78.9 54.1 all-gather.7
  601.4 126.7 all-gather.9
where the time goes:
time: 916 us; the launch traced here: 914 us
  blocking collectives  631 us (69%)
  other arithmetic  146 us (16%)
  waiting for transfers between devices  96.8 us (11%)
  between operations  13.5 us (1%)
  matrix products  12.3 us (1%)
    psum x1, blocking collectives, on_device(): lax.psum(picked, 'seq').astype(jnp.bfloat16).reshape(-1, 3 * head_width)  461 us
    add x127, other arithmetic, combine_parts(): first_out * first_factor[:, None] + second_out * second_factor[:, None]  136 us
    all_gather x2, blocking collectives, merged(): everything = jax.tree.map(lambda part: lax.all_gather(part, axis), value)  130 us
    all_gather x1, waiting for transfers between devices, on_device(): lax.all_gather(normed_part, 'section', axis=1, tiled=True)  55.5 us
    psum x1, waiting for transfers between devices, on_device(): lax.psum((jnp.dot(normed_part, key_weight, preferred_element_type=jnp.flo...  34.5 us
  transfers between devices with their start and end apart: 5, of which 4 were waited for; matrix products, arithmetic and copies ran while one was open for 1% of the time, Pallas kernels for 0%

commit v1 on v0

--- a/solution.py
+++ b/solution.py
@@ -76,6 +76,32 @@
     block_reach,
     header_ids,
 ):
+
+    def _arrange_cards(chunk):
+        tall = jax.lax.axis_index("section")
+        inter = jax.lax.axis_size("section")
+        known, f_next, now = (inter, tall, chunk.shape[1])
+        val = jnp.zeros(
+            [dd * known if dev_i == 1 else dd for dev_i, dd in enumerate(chunk.shape)], chunk.dtype
+        )
+        top = outer = chunk
+        part_next = lax.dynamic_update_slice_in_dim(val, chunk, f_next * now, axis=1)
+        for q in range(1, known // 2 + 1):
+            top = jax.lax.ppermute(
+                top, "section", [(dev_i, (dev_i + 1) % known) for dev_i in range(known)]
+            )
+            part_next = lax.dynamic_update_slice_in_dim(
+                part_next, top, (f_next - q) % known * now, axis=1
+            )
+            if 2 * q < known:
+                outer = jax.lax.ppermute(
+                    outer, "section", [(dev_i, (dev_i - 1) % known) for dev_i in range(known)]
+                )
+                part_next = lax.dynamic_update_slice_in_dim(
+                    part_next, outer, (f_next + q) % known * now, axis=1
+                )
+        return part_next
+
     row_count = hidden.shape[0]
     part_width = hidden.shape[1]
     head_width = key_weight.shape[1]
@@ -90,9 +116,7 @@
     )
     weight_rows = query_weight
     query_sum = jnp.dot(
-        lax.all_gather(normed_part, "section", axis=1, tiled=True),
-        weight_rows,
-        preferred_element_type=jnp.float32,
+        _arrange_cards(normed_part), weight_rows, preferred_element_type=jnp.float32
     )
     key_sum, value_sum = lax.psum(
         (

time: 916 us -> 881 us (0.962)
  waiting for transfers between devices: 96.8 us -> 22.4 us
  blocking collectives: 631 us -> 652 us
    all_gather x1 -> x0, waiting for transfers between devices: 55.5 us -> none  [on_device(): lax.all_gather(normed_part, 'section', axis=1, tiled=True)]
    psum x1, waiting for transfers between devices: 34.5 us -> 0.02 us  [on_device(): lax.psum((jnp.dot(normed_part, key_weight, preferred_element_type=jnp.flo...]
    psum x1, blocking collectives: 17.2 us -> 36.8 us  [on_device(): lax.psum((jnp.dot(normed_part, key_weight, preferred_element_type=jnp.flo...]
    ppermute x0 -> x3, waiting for transfers between devices: none -> 16.2 us  [the longest x2 16.2 us: _arrange_cards(): jax.lax.ppermute(top, 'section', [(dev_i, (dev_i + 1) % known) for dev_i...]
  transfers between devices with their start and end apart: 5 -> 7, of which waited for: 4 -> 3; matrix products, arithmetic and copies ran while one was open for 1% -> 1% of each run, Pallas kernels for 0% -> 0%
where the time goes in v1:
time: 881 us; the launch traced here: 878 us
  blocking collectives  652 us (74%)
  other arithmetic  146 us (17%)
  waiting for transfers between devices  22.4 us (3%)
  starting transfers between devices  15.5 us (2%)
  between operations  13.8 us (2%)
  matrix products  12.1 us (1%)
  local copies, waits for them, and re-layouts  11.9 us (1%)
    psum x1, blocking collectives, on_device(): lax.psum(picked, 'seq').astype(jnp.bfloat16).reshape(-1, 3 * head_width)  463 us
    add x127, other arithmetic, combine_parts(): first_out * first_factor[:, None] + second_out * second_factor[:, None]  136 us
    all_gather x2, blocking collectives, merged(): everything = jax.tree.map(lambda part: lax.all_gather(part, axis), value)  130 us
    psum x1, blocking collectives, on_device(): lax.psum((jnp.dot(normed_part, key_weight, preferred_element_type=jnp.flo...  36.8 us
  transfers between devices with their start and end apart: 7, of which 3 were waited for; matrix products, arithmetic and copies ran while one was open for 1% of the time, Pallas kernels for 0%

profile of v1, /device:TPU:64, one launch (start us, length us, event | category | flops | bytes accessed | tf_op | source)
XLA Modules:
  0.0 878.4 jit_solution(1184531812036470500)
XLA Ops:
  7.3 1.6 fusion.2
  8.9 10.5 %psum.28 = f32[512]{0:T(512)S(1)} all-reduce(f32[512]{0:T(512)S(1)} %fusion.2), channel_id=1, replica_groups=mesh['section'=4,'seq'=128] {'section'}, use_global_device_ids=true, to_apply=%region_2.3 | all-reduce | flops 512 | bytes 4096 | tf_op jit(solution)/shard_map/psum | solution.py:112
  19.4 2.5 broadcast_in_dim.19
  21.9 1.3 constant_dynamic-update-slice_fusion.3
  23.2 1.9 collective-permute-start
  25.1 5.1 collective-permute-start.1
  30.3 1.2 fusion.54
  31.6 1.4 fusion.55
  33.0 16.2 %collective-permute-done = bf16[512,1024]{1,0:T(8,128)(2,1)S(1)} collective-permute-done((bf16[512,1024]{1,0:T(8,128)(2,1)S(1)}, bf16[512,1024]{1,0:T(8,128)(2,1)S(1)}, u32[]{:S(2)}, u32[]{:S(2)}) %collective-permute-start) | collective-permute-done | bytes 1048608 | tf_op jit(solution)/shard_map/ppermute | solution.py:90
  49.2 1.9 collective-permute-start.2
  51.9 36.8 %all-reduce.5 = bf16[512,128]{0,1:T(8,128)(2,1)S(1)} all-reduce(f32[512,128]{0,1:T(8,128)S(1)} %fusion.55), channel_id=1, replica_groups=mesh['section'=4,'seq'=128] {'section'}, use_global_device_ids=true, to_apply=%region_4.5 | all-reduce | flops 65536 | bytes 393216 | tf_op jit(solution)/shard_map/psum | solution.py:121
  90.8 2.5 constant_dynamic-update-slice_fusion.1
  93.3 2.3 constant_dynamic-update-slice_fusion
  95.6 3.7 fusion.53
  101.3 462.8 %all-reduce.6 = bf16[2,128,384]{2,0,1:T(2,128)(2,1)S(1)} all-reduce(f32[2,128,384]{2,0,1:T(2,128)S(1)} %fusion.48), channel_id=1, replica_groups=mesh['section'=4,'seq'=128] {'seq'}, use_global_device_ids=true, to_apply=%region_5.6 | all-reduce | flops 98304 | bytes 589824 | tf_op jit(solution)/shard_map/psum | solution.py:140
  566.1 82.4 %all-gather.3 = f32[128,1,256]{2,1,0:T(1,128)S(1)} all-gather(f32[1,1,256]{2,1,0:T(1,128)S(1)} %bitcast.66), channel_id=2, replica_groups=mesh['section'=4,'seq'=128] {'seq'}, dimensions={0}, use_global_device_ids=true | all-gather | bytes 132096 | tf_op jit(solution)/shard_map/all_gather | solution.py:14
  648.7 47.1 %all-gather.4 = f32[128,1,256]{2,1,0:T(1,128)S(1)} all-gather(f32[1,1,256]{2,1,0:T(1,128)S(1)} %bitcast.67), channel_id=3, replica_groups=mesh['section'=4,'seq'=128] {'seq'}, dimensions={0}, use_global_device_ids=true | all-gather | bytes 132096 | tf_op jit(solution)/shard_map/all_gather | solution.py:14
  695.9 4.5 collective-permute-start.4
  700.4 1.9 collective-permute-start.3
  702.9 5.9 collective-permute-done.3
  712.5 144.2 %while.19 = (s32[]{:T(128)}, f32[256]{0:T(256)S(1)}, f32[256]{0:T(256)S(1)}, f32[256,128]{1,0:T(8,128)S(1)}, f32[128,256]{1,0:T(8,128)S(1)}, /*index=5*/f32[128,...) while((s32[]{:T(128)}, f32[256]{0:T(256)S(1)}, f32[256]{0:T(256)S(1)}, ...), condition=%wide.region_9.10_spmd, body=%wide.region_8.9_spmd.sunk | while | flops 99845 | bytes 407703 | solution.py:20
  713.7 1.1 fusion.70
  715.9 1.1 fusion.70
  718.2 1.1 fusion.70
  720.5 1.1 fusion.70
  722.7 1.1 fusion.70
  723.9 1.1 fusion.70
  725.0 1.1 fusion.70
  726.2 1.1 fusion.70
  727.3 1.1 fusion.70
  728.4 1.1 fusion.70
  730.7 1.1 fusion.70
  733.0 1.1 fusion.70
  735.2 1.1 fusion.70
  737.5 1.1 fusion.70
  739.8 1.1 fusion.70
  742.1 1.1 fusion.70
  744.3 1.1 fusion.70
  745.5 1.1 fusion.70
  746.6 1.1 fusion.70
  747.7 1.1 fusion.70
  748.9 1.1 fusion.70
  750.0 1.1 fusion.70
  752.3 1.1 fusion.70
  754.5 1.1 fusion.70
  756.8 1.1 fusion.70
  857.2 12.6 %all_gather.27 = bf16[512,512]{1,0:T(8,128)(2,1)S(1)} all-gather(bf16[512,128]{1,0:T(8,128)(2,1)S(1)} %bitcast.59), channel_id=1, replica_groups=mesh['section'=4,'seq'=128] {'section'}, dimensions={1}, use_global_device_ids=true | all-gather | bytes 655360 | tf_op jit(solution)/shard_map/all_gather | solution.py:202
  869.8 1.7 convolution_convert_fusion
  (433 shorter events, 125.6 us)
Async XLA Ops:
  6.5 863.3 %copy-start = (bf16[512,1024]{1,0:T(8,128)(2,1)S(1)}, bf16[512,1024]{1,0:T(8,128)(2,1)}, u32[]{:S(2)}) copy-start(bf16[512,1024]{1,0:T(8,128)(2,1)} %param.15) | copy-start | bytes 3145732
  6.5 82.2 %all-reduce.4.cloned.1.call-start = ((), (), s32[]{:S(2)}) async-start(), calls=%async_computation | async-start | bytes 524288 | tf_op jit(solution)/shard_map/psum | solution.py:121
  7.3 14.6 %copy-start.1 = (bf16[512,1024]{1,0:T(8,128)(2,1)S(1)}, bf16[512,1024]{1,0:T(8,128)(2,1)}, u32[]{:S(2)}) copy-start(bf16[512,1024]{1,0:T(8,128)(2,1)} %param.10) | copy-start | bytes 3145732
  21.9 8.4 copy-start.8
  23.2 26.0 %collective-permute-start = (bf16[512,1024]{1,0:T(8,128)(2,1)S(1)}, bf16[512,1024]{1,0:T(8,128)(2,1)S(1)}, u32[]{:S(2)}, u32[]{:S(2)}) collective-permute-start(bf16[512,1024]{1,0:T(8,128)(2,1)S(1)} %get-tuple-element.203), channel_id=1, source_target_pairs={{0,128},{128,256},{256,384},{384,0},{1,129},{129,257},{257,385},{3... | collective-permute-start | bytes 3145736 | tf_op jit(solution)/shard_map/ppermute | solution.py:90
  25.1 65.7 %collective-permute-start.1 = (bf16[512,1024]{1,0:T(8,128)(2,1)S(1)}, bf16[512,1024]{1,0:T(8,128)(2,1)}, u32[]{:S(2)}, u32[]{:S(2)}) collective-permute-start(bf16[512,1024]{1,0:T(8,128)(2,1)S(1)} %get-tuple-element.203), channel_id=1, source_target_pairs={{0,384},{128,0},{256,128},{384,256},{1,385},{129,1},{257,129},{385... | collective-permute-start | bytes 3145736 | tf_op jit(solution)/shard_map/ppermute | solution.py:97
  31.5 680.0 %all-gather.7.cloned.1.call-start = ((), (), s32[]{:S(2)}) async-start(), calls=%async_computation.1 | async-start | bytes 16908288 | tf_op jit(solution)/shard_map/all_gather | solution.py:14
  49.2 44.1 %collective-permute-start.2 = (bf16[512,1024]{1,0:T(8,128)(2,1)S(1)}, bf16[512,1024]{1,0:T(8,128)(2,1)}, u32[]{:S(2)}, u32[]{:S(2)}) collective-permute-start(bf16[512,1024]{1,0:T(8,128)(2,1)S(1)} %collective-permute-done), channel_id=1, source_target_pairs={{0,128},{128,256},{256,384},{384,0},{1,129},{129,257},{257,385},{3... | collective-permute-start | bytes 3145736 | tf_op jit(solution)/shard_map/ppermute | solution.py:90
  90.8 4.8 copy-start.4
  95.6 3.8 copy-start.3
  95.6 3.8 copy-start.7
  99.3 1.6 copy-start.9
  100.5 465.5 %copy-start.10 = (s32[4]{0:T(128)S(1)}, s32[4]{0:T(128)}, u32[]{:S(2)}) copy-start(s32[4]{0:T(128)} %param.16) | copy-start | bytes 52
  648.5 61.5 %copy-start.6 = (f32[128,1,256]{2,1,0:T(1,128)}, f32[128,1,256]{2,1,0:T(1,128)S(1)}, u32[]{:S(2)}) copy-start(f32[128,1,256]{2,1,0:T(1,128)S(1)} %all-gather.3) | copy-start | bytes 393220
  695.8 14.1 %copy-start.5 = (f32[128,1,256]{2,1,0:T(1,128)}, f32[128,1,256]{2,1,0:T(1,128)S(1)}, u32[]{:S(2)}) copy-start(f32[128,1,256]{2,1,0:T(1,128)S(1)} %all-gather.4) | copy-start | bytes 393220
  695.9 7.1 collective-permute-start.4
  700.4 8.4 collective-permute-start.3
  708.9 1.1 copy-start.2
  710.0 1.0 slice-start
  710.9 1.5 slice-start.1
  710.9 1.5 slice-start.2
Sparse Core Ops, SparseCore 0:
  31.6 54.1 all-reduce.3
  565.9 125.5 all-gather.6
